TPU v7x, 256 devices: a whole 4x4x8 slice. The times are simulated.
256 devices in a mesh: tm: 32 (over z, x), coef: 8 (over y, core).
Axes of the slice: x: 4, y: 4, z: 8, core: 2. Of those that a mesh axis runs over, the one named last changes fastest.
Arguments:
- design: float32 [24576, 16384], P('tm', 'coef'), may hold values from -6 to 6
- taps: float32 [384], replicated, may hold values from -0.3125 to 0.3125
Outputs:
- coeffs: float32 [256, 16384], P(None, 'coef')
- reduced: float32 [24576, 16384], P('tm', 'coef')
All inputs are finite; a program needn't handle non-finite values.
Results may differ from a plain program's by a relative error of at most 0.0003.
Values sent between devices are 32-bit elements; how exact they have to be, the bound alone decides.
A program may use at most 64 MiB of HBM per device.

v0:
```python
import functools

import jax
import jax.numpy as jnp
from jax import lax
from jax.experimental import pallas as pl
from jax.experimental.pallas import tpu as pltpu
from jax.sharding import PartitionSpec as P

MESH = pl.DeviceIdType.MESH
F32 = jnp.float32
BF16 = jnp.bfloat16
HIGHEST = lax.Precision.HIGHEST
PANEL = 256
ROWS = 768
REACH = 384
COLUMNS = 2048
CHUNK = 256
CHUNKS = COLUMNS // CHUNK
TILE = 128
NX = 4
PIECES = 8
PIECE_ROWS = 192
PIECE_ORDER = (2, 3, 4, 5, 0, 1, 6, 7)
PLUS = 3
MINUS = 4
SUBS = 2
SUB_ROWS = PANEL // SUBS


def split(value):
    high = value.astype(BF16)
    low = (value - high.astype(F32)).astype(BF16)
    return high, low


def dot(left, right):
    return jnp.dot(left, right, preferred_element_type=F32)


def exact(left, right):
    return jnp.dot(left, right, precision=HIGHEST, preferred_element_type=F32)


def stacked_product(stacked, high, low):
    rows = stacked.shape[0] // 2
    both = dot(stacked, high)
    return both[:rows] + (both[rows:] + dot(stacked[:rows], low))


def build_bands(taps_ref, ahead, behind, behind_split):
    line = jnp.concatenate([taps_ref[...], jnp.zeros((1, TILE), F32)], axis=1)
    band = jnp.broadcast_to(line, (TILE, 4 * TILE))
    row = lax.broadcasted_iota(jnp.int32, (TILE, 4 * TILE), 0)
    step = 1
    while step < TILE:
        band = jnp.where((row // step) % 2 == 1, pltpu.roll(band, step, 1), band)
        step *= 2
    ahead[...] = band
    for block in range(4):
        part = band[:, (3 - block) * TILE : (4 - block) * TILE].T
        columns = slice(block * TILE, (block + 1) * TILE)
        behind[:, columns] = part
        high, low = split(part)
        behind_split[:TILE, columns] = high
        behind_split[TILE:, columns] = low


def eliminate(work, block):
    size = 64
    top = block * size
    rows = slice(top, top + size)
    square = work[rows, top : top + size]
    eye_row = lax.broadcasted_iota(jnp.int32, (size, size), 0)
    eye_column = lax.broadcasted_iota(jnp.int32, (size, size), 1)
    eye = jnp.where(eye_row == eye_column, 1.0, 0.0).astype(F32)
    table = jnp.concatenate([square, eye], axis=1)
    row = lax.broadcasted_iota(jnp.int32, (size, 2 * size), 0)
    for j in range(size):
        column = jnp.broadcast_to(table[:, j : j + 1], (size, 2 * size))
        inverse_root = lax.rsqrt(column[j : j + 1, :])
        pivot = table[j : j + 1, :] * inverse_root
        factor = column * inverse_root
        table = jnp.where(row == j, pivot, jnp.where(row > j, table - factor * pivot, table))
    inverse = table[:, size:]
    panel_rows = exact(inverse, work[rows, :])
    work[rows, :] = panel_rows
    if top + size < PANEL:
        left = panel_rows[:, :PANEL].T[top + size :]
        rest = slice(top + size, PANEL)
        work[rest, :] = work[rest, :] - exact(left, panel_rows)


def exchange_kernel(
    nz, ny, taps_ref, design, white, coeffs, basis,
    slab, halo, wide, panel, cross_left, ahead, behind, behind_split, crossed,
    from_minus, from_plus, across, gathered, gram_own, gram_in, gram_x, gram_all, work,
    load_sem, halo_send, halo_recv, side_send, side_recv, own_sem,
    flow_send, flow_recv, core_send, core_recv,
    gz_send, gz_recv, gx_send, gx_recv, ga_send, ga_recv, gc_send, gc_recv,
    rp_send, rp_recv, rm_send, rm_recv, xs_send, xs_recv, xg_send, xg_recv,
    ap_send, ap_recv, am_send, am_recv,
):
    tm = lax.axis_index("tm")
    coef = lax.axis_index("coef")
    last_tm = nz * NX - 1
    z, x = tm // NX, tm % NX
    y, core = coef // 2, coef % 2
    is_source = coef == 0

    def at(z_to=z, x_to=x, coef_to=coef):
        return (z_to * NX + x_to, coef_to)

    def send(source, target, send_sem, recv_sem, device):
        return pltpu.make_async_remote_copy(
            src_ref=source, dst_ref=target, send_sem=send_sem, recv_sem=recv_sem,
            device_id=device, device_id_type=MESH,
        )

    wrap_up = (x == NX - 1) & (tm < last_tm)
    wrap_down = (x == 0) & (tm > 0)

    for q in range(CHUNKS):
        pltpu.make_async_copy(
            design.at[:, pl.ds(q * CHUNK, CHUNK)], slab.at[q], load_sem.at[q]
        ).start()

    barrier = pltpu.get_barrier_semaphore()

    def greet(device):
        pl.semaphore_signal(barrier, inc=1, device_id=device, device_id_type=MESH)

    for d in range(1, nz):
        greet(at(z_to=(z + d) % nz))
    for d in range(1, NX):
        greet(at(x_to=(x + d) % NX))
    for d in range(1, 2 * ny):
        greet(at(coef_to=(coef + d) % (2 * ny)))
    greetings = nz - 1 + NX - 1 + 2 * ny - 1

    @pl.when(wrap_up)
    def _():
        greet((tm + 1, coef))

    @pl.when(wrap_down)
    def _():
        greet((tm - 1, coef))

    extra = jnp.where(wrap_up, 1, 0) + jnp.where(wrap_down, 1, 0)
    pl.semaphore_wait(barrier, greetings + extra)

    def side(direction, half):
        lanes = pl.ds(half * TILE, TILE)
        if direction == 0:
            source, device, start = design.at[pl.ds(ROWS - REACH, REACH), lanes], (tm + 1, coef), 0
        else:
            source, device, start = design.at[pl.ds(0, REACH), lanes], (tm - 1, coef), REACH + ROWS
        target = wide.at[half, pl.ds(start, REACH), :]
        return send(source, target, side_send.at[direction, half], side_recv.at[direction, half], device)

    def own(half):
        return pltpu.make_async_copy(
            design.at[:, pl.ds(half * TILE, TILE)],
            wide.at[half, pl.ds(REACH, ROWS), :],
            own_sem.at[half],
        )

    def halo_copy(q):
        return send(
            design.at[pl.ds(ROWS - REACH, REACH), pl.ds(q * CHUNK, CHUNK)],
            halo.at[q], halo_send.at[q], halo_recv.at[q], (tm + 1, coef),
        )

    @pl.when(is_source)
    def _():
        for half in range(2):
            own(half).start()

        @pl.when(tm < last_tm)
        def _():
            for half in range(2):
                side(0, half).start()

        @pl.when(tm > 0)
        def _():
            for half in range(2):
                side(1, half).start()

        @pl.when(tm == 0)
        def _():
            wide[:, :REACH, :] = jnp.zeros((2, REACH, TILE), F32)

        @pl.when(tm == last_tm)
        def _():
            wide[:, REACH + ROWS :, :] = jnp.zeros((2, REACH, TILE), F32)

    @pl.when(tm < last_tm)
    def _():
        for q in range(CHUNKS):
            halo_copy(q).start()

    @pl.when(tm == 0)
    def _():
        for q in range(CHUNKS):
            halo[q] = jnp.zeros((REACH, CHUNK), F32)

    build_bands(taps_ref, ahead, behind, behind_split)

    def filtered(block):
        high, low = split(block)
        parts = []
        for i in range(3):
            window = slice(i * TILE, i * TILE + 4 * TILE)
            parts.append(stacked_product(behind_split[...], high[window], low[window]))
        return jnp.concatenate(parts, axis=0)

    def late_rows(q):
        white[q, REACH:, :] = filtered(slab[q])

    def early_rows(q):
        @pl.when(tm > 0)
        def _():
            halo_copy(q).wait_recv()

        white[q, :REACH, :] = filtered(jnp.concatenate([halo[q], slab[q, :REACH, :]], axis=0))

    def piece(half, p):
        return wide.at[half, pl.ds(PIECE_ORDER[p] * PIECE_ROWS, PIECE_ROWS), :]

    def flow(half, p):
        y_to = (y + 1) % ny if half == 0 else (y + ny - 1) % ny
        return send(
            piece(half, p), piece(half, p), flow_send.at[half, p], flow_recv.at[half, p],
            at(coef_to=y_to * 2),
        )

    def to_core(half, p):
        return send(
            piece(half, p), piece(half, p), core_send.at[half, p], core_recv.at[half, p],
            at(coef_to=y * 2 + 1),
        )

    end_of = (ny - 1, 1)
    lag = 2
    for p in range(PIECES + lag):
        if p < PIECES:

            @pl.when(is_source)
            def _():
                if p == 0:
                    for half in range(2):
                        own(half).wait()
                if p == 4:

                    @pl.when(tm > 0)
                    def _():
                        for half in range(2):
                            side(0, half).wait_recv()

                if p == 6:

                    @pl.when(tm < last_tm)
                    def _():
                        for half in range(2):
                            side(1, half).wait_recv()

        for half in range(2):
            if p < PIECES:

                @pl.when((core == 0) & (y != end_of[half]))
                def _():
                    @pl.when(y != 0)
                    def _():
                        flow(half, p).wait_recv()

                    flow(half, p).start()
                    to_core(half, p).start()

            if p >= lag:

                @pl.when((core == 0) & (y == end_of[half]))
                def _():
                    flow(half, p - lag).wait_recv()
                    to_core(half, p - lag).start()

        if p < CHUNKS:
            pltpu.make_async_copy(
                design.at[:, pl.ds(p * CHUNK, CHUNK)], slab.at[p], load_sem.at[p]
            ).wait()
            late_rows(p)

    @pl.when(core == 1)
    def _():
        for p in range(PIECES):
            for half in range(2):
                to_core(half, p).wait_recv()

    def panel_tile(i):
        rows = pl.ds(i * TILE, 4 * TILE)
        window = jnp.concatenate([wide[0, rows, :], wide[1, rows, :]], axis=1)
        return exact(behind[...], window)

    for i in range(ROWS // TILE):
        panel[i * TILE : (i + 1) * TILE, :] = panel_tile(i)
    own_panel = panel[:ROWS, :]
    work[:, :PANEL] = exact(own_panel.T, own_panel)
    for j in range(nz):
        rows = pl.ds(pl.multiple_of(coef * 32 + (j // 2) * 8, 8), 8)
        gram_own[j] = work[rows, (j % 2) * TILE : (j % 2 + 1) * TILE]

    def gram_scatter(d):
        return send(
            gram_own.at[(z + d) % nz], gram_in.at[z], gz_send.at[d], gz_recv.at[z],
            at(z_to=(z + d) % nz),
        )

    def gram_scatter_in(d):
        peer = (z + d) % nz
        return send(gram_own.at[peer], gram_in.at[peer], gz_send.at[d], gz_recv.at[peer], at(z_to=peer))

    def gram_across(d):
        return send(gram_x.at[x], gram_x.at[x], gx_send.at[d], gx_recv.at[x], at(x_to=(x + d) % NX))

    def gram_across_in(d):
        peer = (x + d) % NX
        return send(gram_x.at[peer], gram_x.at[peer], gx_send.at[d], gx_recv.at[peer], at(x_to=peer))

    def gram_gather(d):
        part = gram_all.at[coef, z]
        return send(part, part, ga_send.at[d], ga_recv.at[z], at(z_to=(z + d) % nz))

    def gram_gather_in(d):
        peer = (z + d) % nz
        part = gram_all.at[coef, peer]
        return send(part, part, ga_send.at[d], ga_recv.at[peer], at(z_to=peer))

    def gram_spread(d):
        part = gram_all.at[coef]
        return send(part, part, gc_send.at[d], gc_recv.at[coef], at(coef_to=(coef + d) % (2 * ny)))

    def gram_spread_in(d):
        peer = (coef + d) % (2 * ny)
        part = gram_all.at[peer]
        return send(part, part, gc_send.at[d], gc_recv.at[peer], at(coef_to=peer))

    for d in range(1, nz):
        gram_scatter(d).start()

    for i in range(ROWS // TILE, (ROWS + REACH) // TILE):
        panel[i * TILE : (i + 1) * TILE, :] = jnp.where(tm == last_tm, 0.0, panel_tile(i))
    for i in range(ROWS // TILE):
        columns = slice(i * TILE, (i + 1) * TILE)
        tile = exact(ahead[...], panel[i * TILE : i * TILE + 4 * TILE, :])
        high, low = split(tile.T)
        cross_left[:PANEL, columns] = high
        cross_left[PANEL:, columns] = low

    def cross_chunk(q):
        high, low = split(slab[q])
        crossed[q] = stacked_product(cross_left[...], high, low)

    def sub(s):
        return pl.ds(s * SUB_ROWS, SUB_ROWS)

    def up_index(step):
        return (z + PLUS - step) % nz

    def down_index(step):
        return (z + nz - MINUS + step) % nz

    def reduce_up(step, s):
        return send(
            crossed.at[up_index(step), sub(s), :], from_minus.at[step, sub(s), :],
            rp_send.at[step, s], rp_recv.at[step, s], at(z_to=(z + 1) % nz),
        )

    def reduce_down(step, s):
        return send(
            crossed.at[down_index(step), sub(s), :], from_plus.at[step, sub(s), :],
            rm_send.at[step, s], rm_recv.at[step, s], at(z_to=(z + nz - 1) % nz),
        )

    def start_sums(kind):
        for s in range(SUBS):
            kind(0, s).start()

    def pass_up(step):
        for s in range(SUBS):
            reduce_up(step - 1, s).wait_recv()
            index = up_index(step)
            crossed[index, sub(s), :] = crossed[index, sub(s), :] + from_minus[step - 1, sub(s), :]
            if step < PLUS:
                reduce_up(step, s).start()

    def pass_down(step):
        for s in range(SUBS):
            reduce_down(step - 1, s).wait_recv()
            index = down_index(step)
            crossed[index, sub(s), :] = crossed[index, sub(s), :] + from_plus[step - 1, sub(s), :]
            if step < MINUS:
                reduce_down(step, s).start()

    cross_chunk(down_index(0))
    start_sums(reduce_down)
    cross_chunk(up_index(0))
    start_sums(reduce_up)

    total = gram_own[z]
    for d in range(1, nz):
        gram_scatter_in(d).wait_recv()
        total = total + gram_in[(z + d) % nz]
    gram_x[x] = total
    for d in range(1, NX):
        gram_across(d).start()
    cross_chunk(down_index(1))
    cross_chunk(up_index(1))
    for d in range(1, NX):
        gram_across_in(d).wait_recv()
    total = gram_x[0]
    for i in range(1, NX):
        total = total + gram_x[i]
    gram_all[coef, z] = total
    for d in range(1, nz):
        gram_gather(d).start()
    cross_chunk(down_index(2))
    cross_chunk(up_index(2))
    for d in range(1, nz):
        gram_gather_in(d).wait_recv()
    for d in range(1, 2 * ny):
        gram_spread(d).start()
    cross_chunk(down_index(3))
    cross_chunk(z)
    for d in range(1, 2 * ny):
        gram_spread_in(d).wait_recv()
    for c in range(2 * ny):
        for j in range(nz):
            top = c * 32 + (j // 2) * 8
            work[top : top + 8, (j % 2) * TILE : (j % 2 + 1) * TILE] = gram_all[c, j]
    eye_row = lax.broadcasted_iota(jnp.int32, (PANEL, PANEL), 0)
    eye_column = lax.broadcasted_iota(jnp.int32, (PANEL, PANEL), 1)
    work[:, PANEL:] = jnp.where(eye_row == eye_column, 1.0, 0.0).astype(F32)

    pass_down(1)
    pass_up(1)
    eliminate(work, 0)
    pass_down(2)
    pass_up(2)
    eliminate(work, 1)
    pass_down(3)
    pass_up(3)
    eliminate(work, 2)
    pass_down(4)

    quarter = PANEL // NX

    def x_rows(index):
        return pl.ds(pl.multiple_of(index * quarter, quarter), quarter)

    def across_out(d):
        peer = (x + d) % NX
        return send(
            crossed.at[z, x_rows(peer), :], across.at[x], xs_send.at[d], xs_recv.at[x],
            at(x_to=peer),
        )

    def across_in(d):
        peer = (x + d) % NX
        return send(
            crossed.at[z, x_rows(peer), :], across.at[peer], xs_send.at[d], xs_recv.at[peer],
            at(x_to=peer),
        )

    def gather_out(d):
        part = gathered.at[x_rows(x), :]
        return send(part, part, xg_send.at[d], xg_recv.at[x], at(x_to=(x + d) % NX))

    def gather_in(d):
        peer = (x + d) % NX
        part = gathered.at[x_rows(peer), :]
        return send(part, part, xg_send.at[d], xg_recv.at[peer], at(x_to=peer))

    for d in range(1, NX):
        across_out(d).start()
    eliminate(work, 3)
    total = crossed[z, x_rows(x), :]
    for d in range(1, NX):
        across_in(d).wait_recv()
        total = total + across[(x + d) % NX]
    gathered[x_rows(x), :] = total
    for d in range(1, NX):
        gather_out(d).start()
    basis[...] = exact(panel[:ROWS, :], work[:, PANEL:].T)
    for d in range(1, NX):
        gather_in(d).wait_recv()
    coeffs[z] = exact(work[:, PANEL:], gathered[...])

    def ring_up(step, s):
        part = coeffs.at[(z + nz - step) % nz, sub(s), :]
        return send(part, part, ap_send.at[step, s], ap_recv.at[step, s], at(z_to=(z + 1) % nz))

    def ring_up_in(step, s):
        part = coeffs.at[(z + nz - step) % nz, sub(s), :]
        return send(part, part, ap_send.at[step - 1, s], ap_recv.at[step - 1, s], at(z_to=(z + 1) % nz))

    def ring_down(step, s):
        part = coeffs.at[(z + step) % nz, sub(s), :]
        return send(part, part, am_send.at[step, s], am_recv.at[step, s], at(z_to=(z + nz - 1) % nz))

    def ring_down_in(step, s):
        part = coeffs.at[(z + step) % nz, sub(s), :]
        return send(part, part, am_send.at[step - 1, s], am_recv.at[step - 1, s], at(z_to=(z + 1) % nz))

    up_hops, down_hops = PLUS, MINUS
    for s in range(SUBS):
        ring_up(0, s).start()
        ring_down(0, s).start()
    early_rows(0)
    for step in range(1, max(up_hops, down_hops) + 1):
        for s in range(SUBS):
            if step <= up_hops:
                ring_up_in(step, s).wait_recv()
                if step < up_hops:
                    ring_up(step, s).start()
            if step <= down_hops:
                ring_down_in(step, s).wait_recv()
                if step < down_hops:
                    ring_down(step, s).start()
        for q in range(2 * step - 1, min(2 * step + 1, CHUNKS)):
            early_rows(q)

    @pl.when(tm < last_tm)
    def _():
        for q in range(CHUNKS):
            halo_copy(q).wait_send()

    @pl.when(is_source)
    def _():
        @pl.when(tm < last_tm)
        def _():
            for half in range(2):
                side(0, half).wait_send()

        @pl.when(tm > 0)
        def _():
            for half in range(2):
                side(1, half).wait_send()

    @pl.when(core == 0)
    def _():
        for half in range(2):
            for p in range(PIECES):
                to_core(half, p).wait_send()

            @pl.when(y != end_of[half])
            def _():
                for p in range(PIECES):
                    flow(half, p).wait_send()

    for d in range(1, nz):
        gram_scatter(d).wait_send()
        gram_gather(d).wait_send()
    for d in range(1, NX):
        gram_across(d).wait_send()
        across_out(d).wait_send()
        gather_out(d).wait_send()
    for d in range(1, 2 * ny):
        gram_spread(d).wait_send()
    for s in range(SUBS):
        for step in range(PLUS):
            reduce_up(step, s).wait_send()
        for step in range(MINUS):
            reduce_down(step, s).wait_send()
        for step in range(up_hops):
            ring_up(step, s).wait_send()
        for step in range(down_hops):
            ring_down(step, s).wait_send()


def finish_kernel(scale, white, coeffs, basis, coeffs_out, reduced_out, high, low):
    q = pl.program_id(0)

    @pl.when(q == 0)
    def _():
        top, rest = split(basis[...])
        high[...] = top
        low[...] = rest

    chunk = coeffs[q]
    coeffs_out[...] = chunk
    top, rest = split(chunk)
    product = dot(high[...], top) + (dot(high[...], rest) + dot(low[...], top))
    reduced_out[...] = white[q] - product

    @pl.when((q == 0) & (lax.axis_index("coef") == 0))
    def _():
        reduced_out[...] = basis[...] * scale


def per_device(nz, ny, design, taps):
    dma = pltpu.SemaphoreType.DMA
    vmem = pltpu.VMEM
    white, coeffs, basis = pl.pallas_call(
        functools.partial(exchange_kernel, nz, ny),
        out_shape=(
            vmem((CHUNKS, ROWS, CHUNK), F32),
            vmem((CHUNKS, PANEL, CHUNK), F32),
            vmem((ROWS, PANEL), F32),
        ),
        in_specs=[pl.BlockSpec(memory_space=pltpu.VMEM), pl.BlockSpec(memory_space=pl.ANY)],
        out_specs=[pl.BlockSpec(memory_space=pltpu.VMEM)] * 3,
        scratch_shapes=[
            vmem((CHUNKS, ROWS, CHUNK), F32),
            vmem((CHUNKS, REACH, CHUNK), F32),
            vmem((2, 2 * REACH + ROWS, TILE), F32),
            vmem((ROWS + REACH, PANEL), F32),
            vmem((2 * PANEL, ROWS), BF16),
            vmem((TILE, 4 * TILE), F32),
            vmem((TILE, 4 * TILE), F32),
            vmem((2 * TILE, 4 * TILE), BF16),
            vmem((CHUNKS, PANEL, CHUNK), F32),
            vmem((PLUS, PANEL, CHUNK), F32),
            vmem((MINUS, PANEL, CHUNK), F32),
            vmem((NX, PANEL // NX, CHUNK), F32),
            vmem((PANEL, CHUNK), F32),
            vmem((nz, 8, TILE), F32),
            vmem((nz, 8, TILE), F32),
            vmem((NX, 8, TILE), F32),
            vmem((2 * ny, nz, 8, TILE), F32),
            vmem((PANEL, 2 * PANEL), F32),
            dma((CHUNKS,)), dma((CHUNKS,)), dma((CHUNKS,)),
            dma((2, 2)), dma((2, 2)), dma((2,)),
            dma((2, PIECES)), dma((2, PIECES)), dma((2, PIECES)), dma((2, PIECES)),
            dma((nz,)), dma((nz,)), dma((NX,)), dma((NX,)),
            dma((nz,)), dma((nz,)), dma((2 * ny,)), dma((2 * ny,)),
            dma((PLUS, SUBS)), dma((PLUS, SUBS)), dma((MINUS, SUBS)), dma((MINUS, SUBS)),
            dma((NX,)), dma((NX,)), dma((NX,)), dma((NX,)),
            dma((PLUS, SUBS)), dma((PLUS, SUBS)), dma((MINUS, SUBS)), dma((MINUS, SUBS)),
        ],
        compiler_params=pltpu.CompilerParams(
            collective_id=0, has_side_effects=True, vmem_limit_bytes=40 * 1024 * 1024
        ),
    )(taps.reshape(1, -1), design)
    scale = float((nz * NX * ROWS) ** 0.5)
    keep = pltpu.with_memory_space_constraint
    return pl.pallas_call(
        functools.partial(finish_kernel, scale),
        grid=(CHUNKS,),
        out_shape=(
            jax.ShapeDtypeStruct((PANEL, COLUMNS), F32),
            jax.ShapeDtypeStruct((ROWS, COLUMNS), F32),
        ),
        in_specs=[pl.BlockSpec(memory_space=pltpu.VMEM)] * 3,
        out_specs=[
            pl.BlockSpec((PANEL, CHUNK), lambda q: (0, q)),
            pl.BlockSpec((ROWS, CHUNK), lambda q: (0, q)),
        ],
        scratch_shapes=[vmem((ROWS, PANEL), BF16), vmem((ROWS, PANEL), BF16)],
        compiler_params=pltpu.CompilerParams(vmem_limit_bytes=24 * 1024 * 1024),
    )(keep(white, pltpu.VMEM), keep(coeffs, pltpu.VMEM), keep(basis, pltpu.VMEM))


def solution(mesh):
    nz = mesh.shape["tm"] // NX
    ny = mesh.shape["coef"] // 2
    in_specs = (P("tm", "coef"), P())
    out_specs = (P(None, "coef"), P("tm", "coef"))
    return jax.shard_map(
        functools.partial(per_device, nz, ny), mesh=mesh, in_specs=in_specs,
        out_specs=out_specs, check_vma=False,
    )
```

profile of v0, /device:TPU:16, one launch (start us, length us, event | category | flops | bytes accessed | tf_op | source)
XLA Modules:
  0.0 166.0 jit_solution(2756187127142309313)
XLA Ops:
  0.6 0.7 reshape.7.taps_ref
  1.3 158.1 %shard_map.41 = (f32[8,768,256]{2,1,0:T(8,128)S(1)}, f32[8,256,256]{2,1,0:T(8,128)S(1)}, f32[768,256]{1,0:T(8,128)S(1)}) custom-call(f32[1,384]{1,0:T(1,128)S(1)} %reshape.7.taps_ref, f32[768,2048]{1,0:T(8,128)} %design.1), custom_call_target="tpu_custom_call" | custom-call | tf_op jit(solution)/shard_map/pallas_call | solution.py:602
  159.5 6.5 %shard_map.42 = (f32[256,2048]{1,0:T(8,128)}, f32[768,2048]{1,0:T(8,128)}) custom-call(f32[8,768,256]{2,1,0:T(8,128)S(1)} %get-tuple-element.5.white, f32[8,256,256]{2,1,0:T(8,128)S(1)} %get-tuple-element.6.coeffs, f32[768,256]{1,0:T(8,128)S(1)} %get-tuple-element.7.basis), custom_call_target="tpu_custom_call" | custom-call | tf_op jit(solution)/shard_map/pallas_call | solution.py:645
where the time goes:
time: 166 us
  Pallas kernels  165 us (99%)
    pallas_call x1, Pallas kernels, per_device(): pl.pallas_call(functools.partial(exchange_kernel, nz, ny), out_shape=(vme...  158 us
    pallas_call x1, Pallas kernels, per_device(): pl.pallas_call(functools.partial(finish_kernel, scale), grid=(CHUNKS,), o...  6.5 us

commit v1 on v0

--- a/solution.py
+++ b/solution.py
@@ -21,11 +21,13 @@
 NX = 4
 PIECES = 8
 PIECE_ROWS = 192
-PIECE_ORDER = (2, 3, 4, 5, 0, 1, 6, 7)
+PIECE_ORDER = (2, 3, 4, 5, 0, 6, 1, 7)
 PLUS = 3
 MINUS = 4
 SUBS = 2
 SUB_ROWS = PANEL // SUBS
+FIRST, LAST = (0, 1, 2, 3, 4, 5), (6, 7)
+RELAYED = (3, 4, 5, 7)
 
 
 def split(value):
@@ -92,10 +94,10 @@
 
 
 def exchange_kernel(
-    nz, ny, taps_ref, design, white, coeffs, basis,
-    slab, halo, wide, panel, cross_left, ahead, behind, behind_split, crossed,
+    nz, ny, taps_ref, design, white, coeffs,
+    basis, basis_split, slab, halo, relay, wide, panel, cross_left, ahead, behind, behind_split, crossed,
     from_minus, from_plus, across, gathered, gram_own, gram_in, gram_x, gram_all, work,
-    load_sem, halo_send, halo_recv, side_send, side_recv, own_sem,
+    load_sem, halo_send, halo_recv, relay_send, relay_recv, side_send, side_recv, own_sem,
     flow_send, flow_recv, core_send, core_recv,
     gz_send, gz_recv, gx_send, gx_recv, ga_send, ga_recv, gc_send, gc_recv,
     rp_send, rp_recv, rm_send, rm_recv, xs_send, xs_recv, xg_send, xg_recv,
@@ -120,6 +122,18 @@
     wrap_up = (x == NX - 1) & (tm < last_tm)
     wrap_down = (x == 0) & (tm > 0)
 
+    def own(half):
+        return pltpu.make_async_copy(
+            design.at[:, pl.ds(half * TILE, TILE)],
+            wide.at[half, pl.ds(REACH, ROWS), :],
+            own_sem.at[half],
+        )
+
+    @pl.when(is_source)
+    def _():
+        for half in range(2):
+            own(half).start()
+
     for q in range(CHUNKS):
         pltpu.make_async_copy(
             design.at[:, pl.ds(q * CHUNK, CHUNK)], slab.at[q], load_sem.at[q]
@@ -149,42 +163,86 @@
     extra = jnp.where(wrap_up, 1, 0) + jnp.where(wrap_down, 1, 0)
     pl.semaphore_wait(barrier, greetings + extra)
 
-    def side(direction, half):
-        lanes = pl.ds(half * TILE, TILE)
+    def side(direction, half, part):
+        skip = part * PIECE_ROWS
         if direction == 0:
-            source, device, start = design.at[pl.ds(ROWS - REACH, REACH), lanes], (tm + 1, coef), 0
+            source = wide.at[half, pl.ds(ROWS + skip, PIECE_ROWS), :]
+            device, start = (tm + 1, coef), skip
         else:
-            source, device, start = design.at[pl.ds(0, REACH), lanes], (tm - 1, coef), REACH + ROWS
-        target = wide.at[half, pl.ds(start, REACH), :]
-        return send(source, target, side_send.at[direction, half], side_recv.at[direction, half], device)
-
-    def own(half):
-        return pltpu.make_async_copy(
-            design.at[:, pl.ds(half * TILE, TILE)],
-            wide.at[half, pl.ds(REACH, ROWS), :],
-            own_sem.at[half],
-        )
+            source = wide.at[half, pl.ds(REACH + skip, PIECE_ROWS), :]
+            device, start = (tm - 1, coef), REACH + ROWS + skip
+        target = wide.at[half, pl.ds(start, PIECE_ROWS), :]
+        sems = side_send.at[direction, half, part], side_recv.at[direction, half, part]
+        return send(source, target, *sems, device)
+
+    def halo_source(q):
+        return slab.at[q, pl.ds(ROWS - REACH, REACH), :]
 
     def halo_copy(q):
-        return send(
-            design.at[pl.ds(ROWS - REACH, REACH), pl.ds(q * CHUNK, CHUNK)],
-            halo.at[q], halo_send.at[q], halo_recv.at[q], (tm + 1, coef),
-        )
+        sems = halo_send.at[q], halo_recv.at[q]
+        return send(halo_source(q), halo.at[q], *sems, (tm + 1, coef))
+
+    def relay_out(q):
+        i = RELAYED.index(q)
+        sems = relay_send.at[0, i], relay_recv.at[i]
+        return send(halo_source(q), relay.at[i], *sems, at(z_to=(z + 1) % nz))
+
+    def relay_on(q):
+        i = RELAYED.index(q)
+        sems = relay_send.at[1, i], halo_recv.at[q]
+        return send(relay.at[i], halo.at[q], *sems, at(x_to=(x + 1) % NX))
+
+    wrap_relay = (x == NX - 1) & (z > 0)
+
+    def start_halo(group, direct, relayed, passed):
+        if group:
+
+            @pl.when(x < NX - 1)
+            def _():
+                for q in group:
+                    halo_copy(q).start()
+
+        if relayed:
+
+            @pl.when(wrap_up)
+            def _():
+                for q in relayed:
+                    relay_out(q).start()
+
+        if direct or passed:
+
+            @pl.when(x == NX - 1)
+            def _():
+                for q in sorted(direct + passed):
+                    if q in passed:
+
+                        @pl.when(z > 0)
+                        def _():
+                            relay_out(q).wait_recv()
+                            relay_on(q).start()
+
+                    else:
+
+                        @pl.when(tm < last_tm)
+                        def _():
+                            halo_copy(q).start()
 
     @pl.when(is_source)
     def _():
         for half in range(2):
-            own(half).start()
+            own(half).wait()
 
         @pl.when(tm < last_tm)
         def _():
-            for half in range(2):
-                side(0, half).start()
+            for part in range(2):
+                for half in range(2):
+                    side(0, half, part).start()
 
         @pl.when(tm > 0)
         def _():
-            for half in range(2):
-                side(1, half).start()
+            for part in range(2):
+                for half in range(2):
+                    side(1, half, part).start()
 
         @pl.when(tm == 0)
         def _():
@@ -194,17 +252,10 @@
         def _():
             wide[:, REACH + ROWS :, :] = jnp.zeros((2, REACH, TILE), F32)
 
-    @pl.when(tm < last_tm)
-    def _():
-        for q in range(CHUNKS):
-            halo_copy(q).start()
-
     @pl.when(tm == 0)
     def _():
         for q in range(CHUNKS):
             halo[q] = jnp.zeros((REACH, CHUNK), F32)
-
-    build_bands(taps_ref, ahead, behind, behind_split)
 
     def filtered(block):
         high, low = split(block)
@@ -216,13 +267,26 @@
 
     def late_rows(q):
         white[q, REACH:, :] = filtered(slab[q])
+        white[q, :REACH, :] = jnp.zeros((REACH, CHUNK), F32)
+
+    def late_range(start, end):
+        def one(q, _):
+            late_rows(q)
+            return 0
+
+        lax.fori_loop(start, end, one, 0)
 
     def early_rows(q):
         @pl.when(tm > 0)
         def _():
             halo_copy(q).wait_recv()
 
-        white[q, :REACH, :] = filtered(jnp.concatenate([halo[q], slab[q, :REACH, :]], axis=0))
+        block = jnp.concatenate([halo[q], slab[q, :REACH, :]], axis=0)
+        white[q, :REACH, :] = white[q, :REACH, :] + filtered(block)
+
+    def subtract(q):
+        high, low = split(coeffs[q])
+        white[q] = white[q] - stacked_product(basis_split[...], high, low)
 
     def piece(half, p):
         return wide.at[half, pl.ds(PIECE_ORDER[p] * PIECE_ROWS, PIECE_ROWS), :]
@@ -241,53 +305,57 @@
         )
 
     end_of = (ny - 1, 1)
-    lag = 2
-    for p in range(PIECES + lag):
-        if p < PIECES:
+    own_pieces = 4
+
+    @pl.when(is_source)
+    def _():
+        for p in range(own_pieces):
+            for half in range(2):
+                flow(half, p).start()
+                to_core(half, p).start()
+
+    build_bands(taps_ref, ahead, behind, behind_split)
+    for q in range(CHUNKS):
+        pltpu.make_async_copy(
+            design.at[:, pl.ds(q * CHUNK, CHUNK)], slab.at[q], load_sem.at[q]
+        ).wait()
+    start_halo(FIRST, (0, 1), (3, 4), ())
+
+    @pl.when(core == 1)
+    def _():
+        late_range(0, CHUNKS)
+
+    for p in range(PIECES):
+        if own_pieces <= p < PIECES:
 
             @pl.when(is_source)
             def _():
-                if p == 0:
+                direction, part = p % 2, (p - own_pieces) // 2
+
+                @pl.when((tm > 0) if direction == 0 else (tm < last_tm))
+                def _():
                     for half in range(2):
-                        own(half).wait()
-                if p == 4:
-
-                    @pl.when(tm > 0)
-                    def _():
-                        for half in range(2):
-                            side(0, half).wait_recv()
-
-                if p == 6:
-
-                    @pl.when(tm < last_tm)
-                    def _():
-                        for half in range(2):
-                            side(1, half).wait_recv()
-
-        for half in range(2):
-            if p < PIECES:
-
-                @pl.when((core == 0) & (y != end_of[half]))
-                def _():
-                    @pl.when(y != 0)
-                    def _():
-                        flow(half, p).wait_recv()
-
+                        side(direction, half, part).wait_recv()
+
+                for half in range(2):
                     flow(half, p).start()
                     to_core(half, p).start()
 
-            if p >= lag:
-
-                @pl.when((core == 0) & (y == end_of[half]))
-                def _():
-                    flow(half, p - lag).wait_recv()
-                    to_core(half, p - lag).start()
-
-        if p < CHUNKS:
-            pltpu.make_async_copy(
-                design.at[:, pl.ds(p * CHUNK, CHUNK)], slab.at[p], load_sem.at[p]
-            ).wait()
-            late_rows(p)
+        for half in range(2):
+
+            @pl.when((core == 0) & (y != end_of[half]) & (y != 0))
+            def _():
+                flow(half, p).wait_recv()
+                flow(half, p).start()
+                to_core(half, p).start()
+
+    for half in range(2):
+
+        @pl.when((core == 0) & (y == end_of[half]))
+        def _():
+            for p in range(PIECES):
+                flow(half, p).wait_recv()
+                to_core(half, p).start()
 
     @pl.when(core == 1)
     def _():
@@ -318,12 +386,13 @@
         peer = (z + d) % nz
         return send(gram_own.at[peer], gram_in.at[peer], gz_send.at[d], gz_recv.at[peer], at(z_to=peer))
 
-    def gram_across(d):
-        return send(gram_x.at[x], gram_x.at[x], gx_send.at[d], gx_recv.at[x], at(x_to=(x + d) % NX))
-
-    def gram_across_in(d):
-        peer = (x + d) % NX
-        return send(gram_x.at[peer], gram_x.at[peer], gx_send.at[d], gx_recv.at[peer], at(x_to=peer))
+    def gram_across(step):
+        part = gram_x.at[(x + step) % NX]
+        return send(part, part, gx_send.at[step], gx_recv.at[step], at(x_to=(x + NX - 1) % NX))
+
+    def gram_across_in(step):
+        part = gram_x.at[(x + step + 1) % NX]
+        return send(part, part, gx_send.at[step], gx_recv.at[step], at(x_to=(x + 1) % NX))
 
     def gram_gather(d):
         part = gram_all.at[coef, z]
@@ -345,6 +414,7 @@
 
     for d in range(1, nz):
         gram_scatter(d).start()
+    start_halo((), (), (), (3, 4))
 
     for i in range(ROWS // TILE, (ROWS + REACH) // TILE):
         panel[i * TILE : (i + 1) * TILE, :] = jnp.where(tm == last_tm, 0.0, panel_tile(i))
@@ -410,26 +480,41 @@
         gram_scatter_in(d).wait_recv()
         total = total + gram_in[(z + d) % nz]
     gram_x[x] = total
-    for d in range(1, NX):
-        gram_across(d).start()
+    gram_across(0).start()
     cross_chunk(down_index(1))
     cross_chunk(up_index(1))
-    for d in range(1, NX):
-        gram_across_in(d).wait_recv()
+    cross_chunk(down_index(2))
+    cross_chunk(up_index(2))
+    gram_across_in(0).wait_recv()
+    gram_across(1).start()
+    cross_chunk(down_index(3))
+    cross_chunk(z)
+
+    gram_across_in(1).wait_recv()
+    gram_across(2).start()
+    pass_down(1)
+    pass_up(1)
+    gram_across_in(2).wait_recv()
     total = gram_x[0]
     for i in range(1, NX):
         total = total + gram_x[i]
     gram_all[coef, z] = total
     for d in range(1, nz):
         gram_gather(d).start()
-    cross_chunk(down_index(2))
-    cross_chunk(up_index(2))
+
+    @pl.when(core == 0)
+    def _():
+        late_range(0, CHUNKS // 2)
+
     for d in range(1, nz):
         gram_gather_in(d).wait_recv()
     for d in range(1, 2 * ny):
         gram_spread(d).start()
-    cross_chunk(down_index(3))
-    cross_chunk(z)
+
+    @pl.when(core == 0)
+    def _():
+        late_range(CHUNKS // 2, CHUNKS)
+
     for d in range(1, 2 * ny):
         gram_spread_in(d).wait_recv()
     for c in range(2 * ny):
@@ -440,15 +525,13 @@
     eye_column = lax.broadcasted_iota(jnp.int32, (PANEL, PANEL), 1)
     work[:, PANEL:] = jnp.where(eye_row == eye_column, 1.0, 0.0).astype(F32)
 
-    pass_down(1)
-    pass_up(1)
-    eliminate(work, 0)
     pass_down(2)
     pass_up(2)
-    eliminate(work, 1)
+    start_halo((), (2,), (5, 7), ())
+    eliminate(work, 0)
     pass_down(3)
     pass_up(3)
-    eliminate(work, 2)
+    eliminate(work, 1)
     pass_down(4)
 
     quarter = PANEL // NX
@@ -481,7 +564,7 @@
 
     for d in range(1, NX):
         across_out(d).start()
-    eliminate(work, 3)
+    eliminate(work, 2)
     total = crossed[z, x_rows(x), :]
     for d in range(1, NX):
         across_in(d).wait_recv()
@@ -489,7 +572,7 @@
     gathered[x_rows(x), :] = total
     for d in range(1, NX):
         gather_out(d).start()
-    basis[...] = exact(panel[:ROWS, :], work[:, PANEL:].T)
+    eliminate(work, 3)
     for d in range(1, NX):
         gather_in(d).wait_recv()
     coeffs[z] = exact(work[:, PANEL:], gathered[...])
@@ -514,36 +597,63 @@
     for s in range(SUBS):
         ring_up(0, s).start()
         ring_down(0, s).start()
-    early_rows(0)
+    start_halo(LAST, (6,), (), (5, 7))
+    basis[...] = exact(panel[:ROWS, :], work[:, PANEL:].T)
+    high, low = split(basis[...])
+    basis_split[:ROWS, :] = high
+    basis_split[ROWS:, :] = low
+    subtract(z)
+    for q in (0, 1, 3, 4, 2):
+        early_rows(q)
+    after = ((), (5,), (6,), (7,))
     for step in range(1, max(up_hops, down_hops) + 1):
         for s in range(SUBS):
+            if step <= down_hops:
+                ring_down_in(step, s).wait_recv()
+                if step < down_hops:
+                    ring_down(step, s).start()
             if step <= up_hops:
                 ring_up_in(step, s).wait_recv()
                 if step < up_hops:
                     ring_up(step, s).start()
-            if step <= down_hops:
-                ring_down_in(step, s).wait_recv()
-                if step < down_hops:
-                    ring_down(step, s).start()
-        for q in range(2 * step - 1, min(2 * step + 1, CHUNKS)):
+        if step <= up_hops:
+            subtract((z + nz - step) % nz)
+        for q in after[step - 1]:
             early_rows(q)
-
-    @pl.when(tm < last_tm)
+        if step <= down_hops:
+            subtract((z + step) % nz)
+
+    @pl.when(is_source)
+    def _():
+        white[0] = basis[...] * float((nz * NX * ROWS) ** 0.5)
+
+    @pl.when(x < NX - 1)
     def _():
         for q in range(CHUNKS):
             halo_copy(q).wait_send()
 
+    @pl.when(wrap_up)
+    def _():
+        for q in range(CHUNKS):
+            if q in RELAYED:
+                relay_out(q).wait_send()
+            else:
+                halo_copy(q).wait_send()
+
+    @pl.when(wrap_relay)
+    def _():
+        for q in RELAYED:
+            relay_on(q).wait_send()
+
     @pl.when(is_source)
     def _():
-        @pl.when(tm < last_tm)
-        def _():
-            for half in range(2):
-                side(0, half).wait_send()
-
-        @pl.when(tm > 0)
-        def _():
-            for half in range(2):
-                side(1, half).wait_send()
+        for direction in range(2):
+
+            @pl.when((tm < last_tm) if direction == 0 else (tm > 0))
+            def _():
+                for part in range(2):
+                    for half in range(2):
+                        side(direction, half, part).wait_send()
 
     @pl.when(core == 0)
     def _():
@@ -560,7 +670,7 @@
         gram_scatter(d).wait_send()
         gram_gather(d).wait_send()
     for d in range(1, NX):
-        gram_across(d).wait_send()
+        gram_across(d - 1).wait_send()
         across_out(d).wait_send()
         gather_out(d).wait_send()
     for d in range(1, 2 * ny):
@@ -576,41 +686,35 @@
             ring_down(step, s).wait_send()
 
 
-def finish_kernel(scale, white, coeffs, basis, coeffs_out, reduced_out, high, low):
-    q = pl.program_id(0)
-
-    @pl.when(q == 0)
-    def _():
-        top, rest = split(basis[...])
-        high[...] = top
-        low[...] = rest
-
-    chunk = coeffs[q]
-    coeffs_out[...] = chunk
-    top, rest = split(chunk)
-    product = dot(high[...], top) + (dot(high[...], rest) + dot(low[...], top))
-    reduced_out[...] = white[q] - product
-
-    @pl.when((q == 0) & (lax.axis_index("coef") == 0))
-    def _():
-        reduced_out[...] = basis[...] * scale
+def finish_kernel(white, coeffs, coeffs_out, reduced_out, sems):
+    copies = []
+    for q in range(CHUNKS):
+        columns = pl.ds(q * CHUNK, CHUNK)
+        copies.append(pltpu.make_async_copy(white.at[q], reduced_out.at[:, columns], sems.at[0, q]))
+        copies.append(pltpu.make_async_copy(coeffs.at[q], coeffs_out.at[:, columns], sems.at[1, q]))
+    for copy in copies:
+        copy.start()
+    for copy in copies:
+        copy.wait()
 
 
 def per_device(nz, ny, design, taps):
     dma = pltpu.SemaphoreType.DMA
     vmem = pltpu.VMEM
-    white, coeffs, basis = pl.pallas_call(
+    white, coeffs = pl.pallas_call(
         functools.partial(exchange_kernel, nz, ny),
         out_shape=(
             vmem((CHUNKS, ROWS, CHUNK), F32),
             vmem((CHUNKS, PANEL, CHUNK), F32),
-            vmem((ROWS, PANEL), F32),
         ),
         in_specs=[pl.BlockSpec(memory_space=pltpu.VMEM), pl.BlockSpec(memory_space=pl.ANY)],
-        out_specs=[pl.BlockSpec(memory_space=pltpu.VMEM)] * 3,
+        out_specs=[pl.BlockSpec(memory_space=pltpu.VMEM)] * 2,
         scratch_shapes=[
+            vmem((ROWS, PANEL), F32),
+            vmem((2 * ROWS, PANEL), BF16),
             vmem((CHUNKS, ROWS, CHUNK), F32),
             vmem((CHUNKS, REACH, CHUNK), F32),
+            vmem((len(RELAYED), REACH, CHUNK), F32),
             vmem((2, 2 * REACH + ROWS, TILE), F32),
             vmem((ROWS + REACH, PANEL), F32),
             vmem((2 * PANEL, ROWS), BF16),
@@ -628,7 +732,8 @@
             vmem((2 * ny, nz, 8, TILE), F32),
             vmem((PANEL, 2 * PANEL), F32),
             dma((CHUNKS,)), dma((CHUNKS,)), dma((CHUNKS,)),
-            dma((2, 2)), dma((2, 2)), dma((2,)),
+            dma((2, len(RELAYED))), dma((len(RELAYED),)),
+            dma((2, 2, 2)), dma((2, 2, 2)), dma((2,)),
             dma((2, PIECES)), dma((2, PIECES)), dma((2, PIECES)), dma((2, PIECES)),
             dma((nz,)), dma((nz,)), dma((NX,)), dma((NX,)),
             dma((nz,)), dma((nz,)), dma((2 * ny,)), dma((2 * ny,)),
@@ -640,23 +745,18 @@
             collective_id=0, has_side_effects=True, vmem_limit_bytes=40 * 1024 * 1024
         ),
     )(taps.reshape(1, -1), design)
-    scale = float((nz * NX * ROWS) ** 0.5)
     keep = pltpu.with_memory_space_constraint
     return pl.pallas_call(
-        functools.partial(finish_kernel, scale),
-        grid=(CHUNKS,),
+        finish_kernel,
         out_shape=(
             jax.ShapeDtypeStruct((PANEL, COLUMNS), F32),
             jax.ShapeDtypeStruct((ROWS, COLUMNS), F32),
         ),
-        in_specs=[pl.BlockSpec(memory_space=pltpu.VMEM)] * 3,
-        out_specs=[
-            pl.BlockSpec((PANEL, CHUNK), lambda q: (0, q)),
-            pl.BlockSpec((ROWS, CHUNK), lambda q: (0, q)),
-        ],
-        scratch_shapes=[vmem((ROWS, PANEL), BF16), vmem((ROWS, PANEL), BF16)],
-        compiler_params=pltpu.CompilerParams(vmem_limit_bytes=24 * 1024 * 1024),
-    )(keep(white, pltpu.VMEM), keep(coeffs, pltpu.VMEM), keep(basis, pltpu.VMEM))
+        in_specs=[pl.BlockSpec(memory_space=pltpu.VMEM)] * 2,
+        out_specs=[pl.BlockSpec(memory_space=pl.ANY)] * 2,
+        scratch_shapes=[dma((2, CHUNKS))],
+        compiler_params=pltpu.CompilerParams(vmem_limit_bytes=8 * 1024 * 1024),
+    )(keep(white, pltpu.VMEM), keep(coeffs, pltpu.VMEM))
 
 
 def solution(mesh):

time: 166 us -> 137 us (0.83)
  Pallas kernels: 165 us -> 135 us
    pallas_call x1, Pallas kernels: 158 us -> 131 us  [per_device(): pl.pallas_call(functools.partial(exchange_kernel, nz, ny), out_shape=(vme...]
    pallas_call x1, Pallas kernels: 6.5 us -> 3.41 us  [per_device(): pl.pallas_call(finish_kernel, out_shape=(jax.ShapeDtypeStruct((PANEL, COL...]
where the time goes in v1:
time: 137 us; the launch traced here: 136 us
  Pallas kernels  135 us (99%)
    pallas_call x1, Pallas kernels, per_device(): pl.pallas_call(functools.partial(exchange_kernel, nz, ny), out_shape=(vme...  131 us
    pallas_call x1, Pallas kernels, per_device(): pl.pallas_call(finish_kernel, out_shape=(jax.ShapeDtypeStruct((PANEL, COL...  3.41 us

profile of v1, /device:TPU:16, one launch (start us, length us, event | category | flops | bytes accessed | tf_op | source)
XLA Modules:
  0.0 136.3 jit_solution(10458353495919477116)
XLA Ops:
  0.6 0.7 reshape.7.taps_ref
  1.3 131.4 %shard_map.41 = (f32[8,768,256]{2,1,0:T(8,128)S(1)}, f32[8,256,256]{2,1,0:T(8,128)S(1)}) custom-call(f32[1,384]{1,0:T(1,128)S(1)} %reshape.7.taps_ref, f32[768,2048]{1,0:T(8,128)} %design.1), custom_call_target="tpu_custom_call" | custom-call | tf_op jit(solution)/shard_map/pallas_call | solution.py:704
  132.7 3.4 %shard_map.42 = (f32[256,2048]{1,0:T(8,128)}, f32[768,2048]{1,0:T(8,128)}) custom-call(f32[8,768,256]{2,1,0:T(8,128)S(1)} %get-tuple-element.4.white, f32[8,256,256]{2,1,0:T(8,128)S(1)} %get-tuple-element.5.coeffs), custom_call_target="tpu_custom_call" | custom-call | tf_op jit(solution)/shard_map/pallas_call | solution.py:749

commit v2 on v1

--- a/solution.py
+++ b/solution.py
@@ -319,7 +319,7 @@
         pltpu.make_async_copy(
             design.at[:, pl.ds(q * CHUNK, CHUNK)], slab.at[q], load_sem.at[q]
         ).wait()
-    start_halo(FIRST, (0, 1), (3, 4), ())
+    start_halo(FIRST, (0,), (3, 4), ())
 
     @pl.when(core == 1)
     def _():
@@ -527,7 +527,7 @@
 
     pass_down(2)
     pass_up(2)
-    start_halo((), (2,), (5, 7), ())
+    start_halo((), (1, 2), (5, 7), ())
     eliminate(work, 0)
     pass_down(3)
     pass_up(3)
@@ -603,7 +603,7 @@
     basis_split[:ROWS, :] = high
     basis_split[ROWS:, :] = low
     subtract(z)
-    for q in (0, 1, 3, 4, 2):
+    for q in (0, 3, 4, 1, 2):
         early_rows(q)
     after = ((), (5,), (6,), (7,))
     for step in range(1, max(up_hops, down_hops) + 1):

time: 137 us -> 138 us (level)
  no operation moved by 1% of the time
where the time goes in v2:
time: 138 us; the launch traced here: 136 us
  Pallas kernels  135 us (98%)
    pallas_call x1, Pallas kernels, per_device(): pl.pallas_call(functools.partial(exchange_kernel, nz, ny), out_shape=(vme...  132 us
    pallas_call x1, Pallas kernels, per_device(): pl.pallas_call(finish_kernel, out_shape=(jax.ShapeDtypeStruct((PANEL, COL...  3.41 us

profile of v2, /device:TPU:16, one launch (start us, length us, event | category | flops | bytes accessed | tf_op | source)
XLA Modules:
  0.0 136.4 jit_solution(7394395897365591652)
XLA Ops:
  0.6 0.7 reshape.7.taps_ref
  1.3 131.5 %shard_map.41 = (f32[8,768,256]{2,1,0:T(8,128)S(1)}, f32[8,256,256]{2,1,0:T(8,128)S(1)}) custom-call(f32[1,384]{1,0:T(1,128)S(1)} %reshape.7.taps_ref, f32[768,2048]{1,0:T(8,128)} %design.1), custom_call_target="tpu_custom_call" | custom-call | tf_op jit(solution)/shard_map/pallas_call | solution.py:704
  132.8 3.4 %shard_map.42 = (f32[256,2048]{1,0:T(8,128)}, f32[768,2048]{1,0:T(8,128)}) custom-call(f32[8,768,256]{2,1,0:T(8,128)S(1)} %get-tuple-element.4.white, f32[8,256,256]{2,1,0:T(8,128)S(1)} %get-tuple-element.5.coeffs), custom_call_target="tpu_custom_call" | custom-call | tf_op jit(solution)/shard_map/pallas_call | solution.py:749
